TPU v7x, 128 devices: a whole 4x4x4 slice. The times are simulated.
128 devices in a mesh: row: 8 (over y, core), col: 16 (over z, x).
Axes of the slice: x: 4, y: 4, z: 4, core: 2. Of those that a mesh axis runs over, the one named last changes fastest.
Arguments:
- block_x: float32 [64, 98304], P(None, ('row', 'col')), may hold values from -6 to 6
- block_p: float32 [64, 98304], P(None, ('row', 'col')), may hold values from -6 to 6
- tile_rows: int32 [8, 16, 576], P('row', 'col'), may hold values from 0 to 95, as said below
- tile_cols: int32 [8, 16, 576], P('row', 'col'), may hold values from 0 to 47, as said below
- tile_count: int32 [8, 16], P('row', 'col'), may hold values from 1 to 576, as said below
- tile_vals: bfloat16 [8, 16, 576, 128, 128], P('row', 'col'), may hold values from -0.125 to 0.125
Outputs:
- residual: float32 [64, 98304], P(None, ('row', 'col'))
- image_r: float32 [64, 98304], P(None, ('row', 'col'))
- gram_a: float32 [192, 192], replicated
- gram_b: float32 [192, 192], replicated
Inputs may be any that keep to these rules, and one draw needn't show every extreme that they name: `tile_rows`: within one grid cell the live slots name distinct tiles, all with i <= j; slots at and beyond the cell's count are ignored. `tile_cols`: paired with tile_rows slot by slot. `tile_count`: some grid cell is full in every draw.
All inputs are finite; a program needn't handle non-finite values.
Results may differ from a plain program's by a relative error of at most 0.0035.
Values may be sent and summed in bfloat16 or wider, within the bound.
A program may use at most 128 MiB of HBM per device.

v0:
```python
import math
import jax
import jax.numpy as jnp
from jax import lax
from jax.sharding import PartitionSpec as P


def apply_graph(vectors, tile_rows, tile_cols, live_count, tile_vals):
    vec_width = vectors.shape[0]
    tile_size = tile_vals.shape[-1]
    row_range = lax.all_gather(vectors, "col", axis=1, tiled=True)
    col_group = lax.all_gather(vectors, "row", axis=1, tiled=True)
    row_blocks = row_range.reshape(vec_width, -1, tile_size)
    col_blocks = col_group.reshape(vec_width, -1, tile_size)
    group_size = math.gcd(tile_vals.shape[0], 64)
    offsets = jnp.arange(group_size, dtype=jnp.int32)
    turn_count = (live_count + group_size - 1) // group_size

    def slot_group(turn_index):
        first_slot = turn_index * group_size
        row_index = lax.dynamic_slice_in_dim(tile_rows, first_slot, group_size)
        col_index = lax.dynamic_slice_in_dim(tile_cols, first_slot, group_size)
        values = lax.dynamic_slice_in_dim(tile_vals, first_slot, group_size, 0)
        live_slots = first_slot + offsets < live_count
        return (row_index, col_index, values, live_slots)

    def turn(turn_index, totals):
        row_totals, col_totals = totals
        row_index, col_index, values, live_slots = slot_group(turn_index)
        values = jnp.where(live_slots[:, None, None], values, jnp.zeros_like(values))
        col_inputs = jnp.take(col_blocks, col_index, axis=1)
        row_inputs = jnp.take(row_blocks, row_index, axis=1)
        forward = jnp.einsum("wgb,gab->wga", col_inputs, values, preferred_element_type=jnp.float32)
        backward = jnp.einsum(
            "wga,gab->wgb", row_inputs, values, preferred_element_type=jnp.float32
        )
        return (row_totals.at[:, row_index].add(forward), col_totals.at[:, col_index].add(backward))

    start_rows = jnp.zeros(row_blocks.shape, jnp.float32)
    start_cols = jnp.zeros(col_blocks.shape, jnp.float32)
    row_totals, col_totals = lax.fori_loop(0, turn_count, turn, (start_rows, start_cols))
    own_rows = lax.psum_scatter(
        row_totals.reshape(vec_width, -1), "col", scatter_dimension=1, tiled=True
    )
    own_cols = lax.psum_scatter(
        col_totals.reshape(vec_width, -1), "row", scatter_dimension=1, tiled=True
    )
    return own_rows + own_cols


def per_device(block_x, block_p, tile_rows, tile_cols, tile_count, tile_vals):
    highest = lax.Precision.HIGHEST
    width_k = block_x.shape[0]
    node_count = block_x.shape[1] * lax.axis_size("row") * lax.axis_size("col")
    slot_rows = tile_rows[0, 0]
    slot_cols = tile_cols[0, 0]
    live_count = tile_count[0, 0]
    slot_vals = tile_vals[0, 0]

    def product(left, right):
        return (
            jnp.dot(left, right.T, precision=highest, preferred_element_type=jnp.float32)
            / node_count
        )

    gram_x = lax.psum(product(block_x, block_x), ("row", "col"))
    cholesky_factor = jnp.linalg.cholesky(gram_x)
    orthonormal = lax.linalg.triangular_solve(cholesky_factor, block_x, left_side=True, lower=True)
    ortho_low = orthonormal.astype(jnp.bfloat16)
    dir_low = block_p.astype(jnp.bfloat16)
    both_images = apply_graph(
        jnp.concatenate([ortho_low, dir_low], axis=0), slot_rows, slot_cols, live_count, slot_vals
    )
    image_x = both_images[:width_k]
    image_p = both_images[width_k:]
    rayleigh = lax.psum(product(orthonormal, image_x), ("row", "col"))
    residual = image_x - jnp.dot(
        rayleigh.T, orthonormal, precision=highest, preferred_element_type=jnp.float32
    )
    residual_low = residual.astype(jnp.bfloat16)
    image_r = apply_graph(residual_low, slot_rows, slot_cols, live_count, slot_vals)
    basis = jnp.concatenate([orthonormal, residual, block_p], axis=0)
    images = jnp.concatenate([image_x, image_r, image_p], axis=0)
    gram_a, gram_b = lax.psum((product(basis, images), product(basis, basis)), ("row", "col"))
    return (residual, image_r, gram_a, gram_b)


def solution(mesh):
    in_specs = (
        P(None, ("row", "col")),
        P(None, ("row", "col")),
        P("row", "col", None),
        P("row", "col", None),
        P("row", "col"),
        P("row", "col", None, None, None),
    )
    out_specs = (P(None, ("row", "col")), P(None, ("row", "col")), P(), P())
    return jax.shard_map(
        per_device, mesh=mesh, in_specs=in_specs, out_specs=out_specs, check_vma=False
    )
```

profile of v0, /device:TPU:1, one launch (start us, length us, event | category | flops | bytes accessed | tf_op | source)
XLA Modules:
  0.0 1301.9 jit_solution(9293041823528149920)
XLA Ops:
  8.4 68.9 %psum.28 = f32[64,64]{0,1:T(8,128)S(1)} all-reduce(f32[64,64]{0,1:T(8,128)S(1)} %convolution_multiply_fusion.3), channel_id=1, replica_groups=mesh['row'=8,'col'=16] {'row','col'}, use_global_device_ids=true, to_apply=%region_0.0 | all-reduce | flops 4096 | bytes 32768 | tf_op jit(solution)/shard_map/psum | solution.py:66
  77.4 5.8 cholesky.16
  84.6 4.9 custom-call.6
  93.1 19.8 %all-gather.4.cloned.1.call-done = bf16[128,6144]{1,0:T(8,128)(2,1)} async-done(((bf16[128,768]{1,0:T(8,128)(2,1)}), bf16[128,6144]{1,0:T(8,128)(2,1)}) %all-gather.4.cloned.1.call-update) | async-done | bytes 1572880 | tf_op jit(solution)/shard_map/all_gather | solution.py:12
  115.9 47.5 %all-gather.6.cloned.1.call-done = bf16[128,12288]{1,0:T(8,128)(2,1)} async-done(((bf16[128,768]{1,0:T(8,128)(2,1)}), bf16[128,12288]{1,0:T(8,128)(2,1)}) %all-gather.6.cloned.1.call-update) | async-done | bytes 3145744 | tf_op jit(solution)/shard_map/all_gather | solution.py:11
  163.3 4.5 copy_bitcast_fusion.3
  171.6 290.6 %while.26 = (s32[]{:T(128)}, f32[128,96,128]{2,0,1:T(8,128)}, f32[128,48,128]{2,0,1:T(8,128)S(1)}, s32[]{:T(128)}, s32[576]{0:T(1024)S(1)}, /*index=5*/s32[]{:T(...) while((s32[]{:T(128)}, f32[128,96,128]{2,0,1:T(8,128)}, ...), condition=%wide.region_6.7_spmd.clone, body=%wide.region_3.6_spmd.clone.sunk | while | flops 543165312 | bytes 50343056 | solution.py:41
  175.9 5.8 fusion.80
  181.7 13.6 %scatter_fusion = f32[128,96,128]{2,0,1:T(8,128)} fusion(f32[128,96,128]{2,0,1:T(8,128)} %get-tuple-element.407, s32[64]{0:T(128)S(1)} %get-tuple-element.374, f32[64,128,128]{2,1,0:T(8,128)} %fusion.80), kind=kCustom, calls=%fused_computation.4.clone.clone.1 | custom fusion | flops 1048576 | bytes 12583168 | tf_op jit(solution)/shard_map/while/body/scatter-add | solution.py:37
  195.4 4.0 gather_fusion.1
  199.4 4.9 fusion.81
  204.3 8.8 scatter_fusion.1
  217.4 5.8 fusion.80
  223.2 13.6 %scatter_fusion = f32[128,96,128]{2,0,1:T(8,128)} fusion(f32[128,96,128]{2,0,1:T(8,128)} %get-tuple-element.407, s32[64]{0:T(128)S(1)} %get-tuple-element.374, f32[64,128,128]{2,1,0:T(8,128)} %fusion.80), kind=kCustom, calls=%fused_computation.4.clone.clone.1 | custom fusion | flops 1048576 | bytes 12583168 | tf_op jit(solution)/shard_map/while/body/scatter-add | solution.py:37
  236.9 4.0 gather_fusion.1
  240.9 4.9 fusion.81
  245.8 8.8 scatter_fusion.1
  258.9 5.8 fusion.80
  264.8 13.6 %scatter_fusion = f32[128,96,128]{2,0,1:T(8,128)} fusion(f32[128,96,128]{2,0,1:T(8,128)} %get-tuple-element.407, s32[64]{0:T(128)S(1)} %get-tuple-element.374, f32[64,128,128]{2,1,0:T(8,128)} %fusion.80), kind=kCustom, calls=%fused_computation.4.clone.clone.1 | custom fusion | flops 1048576 | bytes 12583168 | tf_op jit(solution)/shard_map/while/body/scatter-add | solution.py:37
  278.4 4.0 gather_fusion.1
  282.4 4.9 fusion.81
  287.3 8.8 scatter_fusion.1
  300.5 5.8 fusion.80
  306.3 13.5 %scatter_fusion = f32[128,96,128]{2,0,1:T(8,128)} fusion(f32[128,96,128]{2,0,1:T(8,128)} %get-tuple-element.407, s32[64]{0:T(128)S(1)} %get-tuple-element.374, f32[64,128,128]{2,1,0:T(8,128)} %fusion.80), kind=kCustom, calls=%fused_computation.4.clone.clone.1 | custom fusion | flops 1048576 | bytes 12583168 | tf_op jit(solution)/shard_map/while/body/scatter-add | solution.py:37
  319.8 4.0 gather_fusion.1
  323.9 4.9 fusion.81
  328.8 8.8 scatter_fusion.1
  341.9 5.8 fusion.80
  347.7 13.6 %scatter_fusion = f32[128,96,128]{2,0,1:T(8,128)} fusion(f32[128,96,128]{2,0,1:T(8,128)} %get-tuple-element.407, s32[64]{0:T(128)S(1)} %get-tuple-element.374, f32[64,128,128]{2,1,0:T(8,128)} %fusion.80), kind=kCustom, calls=%fused_computation.4.clone.clone.1 | custom fusion | flops 1048576 | bytes 12583168 | tf_op jit(solution)/shard_map/while/body/scatter-add | solution.py:37
  361.3 4.0 gather_fusion.1
  365.4 4.9 fusion.81
  370.3 8.8 scatter_fusion.1
  383.4 5.8 fusion.80
  389.2 13.6 %scatter_fusion = f32[128,96,128]{2,0,1:T(8,128)} fusion(f32[128,96,128]{2,0,1:T(8,128)} %get-tuple-element.407, s32[64]{0:T(128)S(1)} %get-tuple-element.374, f32[64,128,128]{2,1,0:T(8,128)} %fusion.80), kind=kCustom, calls=%fused_computation.4.clone.clone.1 | custom fusion | flops 1048576 | bytes 12583168 | tf_op jit(solution)/shard_map/while/body/scatter-add | solution.py:37
  406.9 4.9 fusion.81
  411.8 8.8 scatter_fusion.1
  424.9 5.8 fusion.80
  430.7 13.6 %scatter_fusion = f32[128,96,128]{2,0,1:T(8,128)} fusion(f32[128,96,128]{2,0,1:T(8,128)} %get-tuple-element.407, s32[64]{0:T(128)S(1)} %get-tuple-element.374, f32[64,128,128]{2,1,0:T(8,128)} %fusion.80), kind=kCustom, calls=%fused_computation.4.clone.clone.1 | custom fusion | flops 1048576 | bytes 12583168 | tf_op jit(solution)/shard_map/while/body/scatter-add | solution.py:37
  448.4 4.9 fusion.81
  453.3 8.8 scatter_fusion.1
  464.2 6.1 copy_bitcast_fusion
  470.4 106.4 %reduce-scatter.7.cloned.1.call-done = f32[128,768]{1,0:T(8,128)} async-done(((f32[128,6144]{1,0:T(8,128)}), f32[128,768]{1,0:T(8,128)}) %reduce-scatter.7.cloned.1.call-update) | async-done | bytes 393232 | tf_op jit(solution)/shard_map/reduce_scatter | solution.py:45
  576.8 85.4 %reduce-scatter.5.cloned.1.call-done = f32[128,768]{1,0:T(8,128)} async-done(((f32[128,12288]{1,0:T(8,128)}), f32[128,768]{1,0:T(8,128)}) %reduce-scatter.5.cloned.1.call-update) | async-done | bytes 393232 | tf_op jit(solution)/shard_map/reduce_scatter | solution.py:42
  663.6 65.7 %psum.29 = f32[64,64]{0,1:T(8,128)S(1)} all-reduce(f32[64,64]{0,1:T(8,128)S(1)} %convolution_multiply_fusion.2), channel_id=1, replica_groups=mesh['row'=8,'col'=16] {'row','col'}, use_global_device_ids=true, to_apply=%region_9.10 | all-reduce | flops 4096 | bytes 32768 | tf_op jit(solution)/shard_map/psum | solution.py:76
  730.4 14.3 %all_gather.14 = bf16[64,6144]{1,0:T(8,128)(2,1)S(1)} all-gather(bf16[64,768]{1,0:T(8,128)(2,1)} %get-tuple-element.250), channel_id=1, replica_groups=mesh['row'=8,'col'=16] {'row'}, dimensions={1}, use_global_device_ids=true | all-gather | bytes 884736 | tf_op jit(solution)/shard_map/all_gather | solution.py:12
  745.8 24.0 %all-gather.8.cloned.1.call-done = bf16[64,12288]{1,0:T(8,128)(2,1)} async-done(((bf16[64,768]{1,0:T(8,128)(2,1)}), bf16[64,12288]{1,0:T(8,128)(2,1)}) %all-gather.8.cloned.1.call-update) | async-done | bytes 1572880 | tf_op jit(solution)/shard_map/all_gather | solution.py:11
  776.2 198.4 %while.27 = (s32[]{:T(128)}, f32[64,96,128]{2,0,1:T(8,128)}, f32[64,48,128]{2,0,1:T(8,128)}, s32[]{:T(128)}, s32[576]{0:T(1024)S(1)}, /*index=5*/s32[]{:T(128)},...) while((s32[]{:T(128)}, f32[64,96,128]{2,0,1:T(8,128)}, ...), condition=%wide.region_13.14_spmd.clone, body=%wide.region_10.13_spmd.clone.sunk | while | flops 272632704 | bytes 27274384 | solution.py:41
  782.0 9.0 scatter_fusion.2
  795.5 9.0 scatter_fusion.3
  810.4 9.0 scatter_fusion.2
  823.9 9.0 scatter_fusion.3
  838.7 9.0 scatter_fusion.2
  852.2 9.0 scatter_fusion.3
  867.0 9.0 scatter_fusion.2
  880.5 9.0 scatter_fusion.3
  895.3 9.0 scatter_fusion.2
  908.9 9.0 scatter_fusion.3
  923.6 9.1 scatter_fusion.2
  937.2 9.0 scatter_fusion.3
  952.0 9.0 scatter_fusion.2
  965.5 9.0 scatter_fusion.3
  981.7 80.2 %reduce-scatter.11.cloned.1.call-done = f32[64,768]{1,0:T(8,128)} async-done(((f32[64,6144]{1,0:T(8,128)}), f32[64,768]{1,0:T(8,128)}) %reduce-scatter.11.cloned.1.call-update) | async-done | bytes 196624 | tf_op jit(solution)/shard_map/reduce_scatter | solution.py:45
  1061.9 79.4 %reduce-scatter.9.cloned.1.call-done = f32[64,768]{1,0:T(8,128)} async-done(((f32[64,12288]{1,0:T(8,128)}), f32[64,768]{1,0:T(8,128)}) %reduce-scatter.9.cloned.1.call-update) | async-done | bytes 196624 | tf_op jit(solution)/shard_map/reduce_scatter | solution.py:42
  1143.7 148.1 %all-reduce.3.cloned.1.call-done = (f32[192,192]{1,0:T(8,128)}, f32[192,192]{1,0:T(8,128)}) async-done(((f32[192,192]{1,0:T(8,128)}, f32[192,192]{1,0:T(8,128)}), (f32[192,192]{1,0:T(8,128)}, f32[192,192]{1,0:T(8,128)})) %all-reduce.3.cloned.1.call-update) | async-done | bytes 294928 | tf_op jit(solution)/shard_map/psum | solution.py:84
  (159 shorter events, 147.3 us)
Async XLA Ops:
  7.2 0.9 copy-start
  7.2 85.8 %copy-start.8 = (s32[1,1,576]{2,1,0:T(1,128)S(1)}, s32[1,1,576]{2,1,0:T(1,128)}, u32[]{:S(2)}) copy-start(s32[1,1,576]{2,1,0:T(1,128)} %param.12) | copy-start | bytes 6916
  7.2 85.8 %copy-start.9 = (s32[1,1,576]{2,1,0:T(1,128)S(1)}, s32[1,1,576]{2,1,0:T(1,128)}, u32[]{:S(2)}) copy-start(s32[1,1,576]{2,1,0:T(1,128)} %param.13) | copy-start | bytes 6916
  7.2 105.7 %all-gather.4.cloned.1.call-start = ((), (), s32[]{:S(2)}) async-start(), calls=%async_computation.4 | async-start | bytes 1769472 | tf_op jit(solution)/shard_map/all_gather | solution.py:12
  91.5 71.8 %all-gather.6.cloned.1.call-start = ((), (), s32[]{:S(2)}) async-start(), calls=%async_computation.5 | async-start | bytes 3342336 | tf_op jit(solution)/shard_map/all_gather | solution.py:11
  92.3 484.5 %reduce-scatter.7.cloned.1.call-start = ((), (), s32[]{:S(2)}) async-start(), calls=%async_computation.7 | async-start | bytes 3538944 | tf_op jit(solution)/shard_map/reduce_scatter | solution.py:45
  464.2 198.0 %reduce-scatter.5.cloned.1.call-start = ((), (), s32[]{:S(2)}) async-start(), calls=%async_computation.6 | async-start | bytes 6684672 | tf_op jit(solution)/shard_map/reduce_scatter | solution.py:42
  470.3 299.4 %all-gather.8.cloned.1.call-start = ((), (), s32[]{:S(2)}) async-start(), calls=%async_computation.8 | async-start | bytes 1671168 | tf_op jit(solution)/shard_map/all_gather | solution.py:11
  663.3 109.5 %copy-start.3 = (f32[128,768]{1,0:T(8,128)}, f32[128,768]{1,0:T(8,128)S(1)}, u32[]{:S(2)}) copy-start(f32[128,768]{1,0:T(8,128)S(1)} %add.116) | copy-start | bytes 1179652
  730.3 331.6 %reduce-scatter.11.cloned.1.call-start = ((), (), s32[]{:S(2)}) async-start(), calls=%async_computation.10 | async-start | bytes 1769472 | tf_op jit(solution)/shard_map/reduce_scatter | solution.py:45
  974.6 2.9 copy-start.2
  977.4 163.9 %reduce-scatter.9.cloned.1.call-start = ((), (), s32[]{:S(2)}) async-start(), calls=%async_computation.9 | async-start | bytes 3342336 | tf_op jit(solution)/shard_map/reduce_scatter | solution.py:42
  979.3 0.9 copy-start.5
  979.3 1.0 copy-start.6
  979.3 2.3 copy-start.4
  979.3 312.4 %all-reduce.3.cloned.1.call-start = ((), (), s32[]{:S(2)}) async-start(), calls=%async_computation.11 | async-start | bytes 786432 | tf_op jit(solution)/shard_map/psum | solution.py:84
  980.3 314.7 %copy-start.1 = (f32[64,768]{1,0:T(8,128)S(1)}, f32[64,768]{1,0:T(8,128)}, u32[]{:S(2)}) copy-start(f32[64,768]{1,0:T(8,128)} %param.10) | copy-start | bytes 589828
  1142.3 152.7 %copy-start.7 = (f32[64,768]{1,0:T(8,128)}, f32[64,768]{1,0:T(8,128)S(1)}, u32[]{:S(2)}) copy-start(f32[64,768]{1,0:T(8,128)S(1)} %add.117) | copy-start | bytes 589828
Sparse Core Ops, SparseCore 0:
  91.7 21.1 all-gather.3
  115.6 47.6 all-gather.5
  464.3 112.4 reduce-scatter.6
  580.0 82.0 reduce-scatter.4
  730.4 39.2 all-gather.7
  977.5 84.3 reduce-scatter.10
  1065.2 76.0 reduce-scatter.8
  1146.6 145.1 all-reduce.2
where the time goes:
time: 1310 us; the launch traced here: 1300 us
  waiting for transfers between devices  591 us (45%)
  other arithmetic  309 us (24%)
  blocking collectives  149 us (11%)
  local copies, waits for them, and re-layouts  118 us (9%)
  matrix products  118 us (9%)
  between operations  15 us (1%)
    reduce_scatter x2, waiting for transfers between devices, apply_graph(): lax.psum_scatter(col_totals.reshape(vec_width, -1), 'row', scatter_dimens...  187 us
    reduce_scatter x2, waiting for transfers between devices, apply_graph(): lax.psum_scatter(row_totals.reshape(vec_width, -1), 'col', scatter_dimens...  165 us
    scatter-add x14, other arithmetic, turn(): row_totals.at[:, row_index].add(forward)  158 us
    psum x1, waiting for transfers between devices, per_device(): lax.psum((product(basis, images), product(basis, basis)), ('row', 'col'))  148 us
    scatter-add x14, other arithmetic, turn(): col_totals.at[:, col_index].add(backward)  125 us
    all_gather x2, waiting for transfers between devices, apply_graph(): row_range = lax.all_gather(vectors, 'col', axis=1, tiled=True)  71.4 us
    psum x1, blocking collectives, per_device(): gram_x = lax.psum(product(block_x, block_x), ('row', 'col'))  68.9 us
    psum x1, blocking collectives, per_device(): rayleigh = lax.psum(product(orthonormal, image_x), ('row', 'col'))  65.7 us
  transfers between devices with their start and end apart: 8, of which 8 were waited for; matrix products, arithmetic and copies ran while one was open for 1% of the time, Pallas kernels for 0%

commit v1 on v0

--- a/solution.py
+++ b/solution.py
@@ -5,10 +5,23 @@
 from jax.sharding import PartitionSpec as P
 
 
+def in_order(blocks, dim):
+    lengths = list(blocks.shape[1:])
+    lengths[dim] *= blocks.shape[0]
+    return jnp.moveaxis(blocks, 0, dim).reshape(lengths)
+
+
 def apply_graph(vectors, tile_rows, tile_cols, live_count, tile_vals):
     vec_width = vectors.shape[0]
     tile_size = tile_vals.shape[-1]
-    row_range = lax.all_gather(vectors, "col", axis=1, tiled=True)
+    count = lax.axis_size("col")
+    forward_2 = [(i, (i + 1) % count) for i in range(count)]
+    parts = [vectors]
+    while len(parts) < count:
+        parts.append(lax.ppermute(parts[-1], "col", forward_2))
+    place = lax.axis_index("col")
+    parts = jnp.stack(parts)[(place - jnp.arange(count)) % count]
+    row_range = in_order(parts, 1)
     col_group = lax.all_gather(vectors, "row", axis=1, tiled=True)
     row_blocks = row_range.reshape(vec_width, -1, tile_size)
     col_blocks = col_group.reshape(vec_width, -1, tile_size)

time: 1310 us -> 1470 us (1.12)
  waiting for transfers between devices: 591 us -> 720 us
  local copies, waits for them, and re-layouts: 118 us -> 147 us
    ppermute x0 -> x30, waiting for transfers between devices: none -> 205 us  [apply_graph(): parts.append(lax.ppermute(parts[-1], 'col', forward_2))]
    all_gather x2 -> x0, waiting for transfers between devices: 71.4 us -> none  [apply_graph(): row_range = lax.all_gather(vectors, 'col', axis=1, tiled=True)]
    all_gather x1, waiting for transfers between devices: 19.8 us -> 0.01 us  [apply_graph(): col_group = lax.all_gather(vectors, 'row', axis=1, tiled=True)]
    unnamed x26 -> x54, local copies, waits for them, and re-layouts: 16.6 us -> 34.5 us
    reduce_scatter x2, waiting for transfers between devices: 187 us -> 202 us  [apply_graph(): lax.psum_scatter(col_totals.reshape(vec_width, -1), 'row', scatter_dimens...]
  transfers between devices with their start and end apart: 8 -> 36, of which waited for: 8 -> 35; matrix products, arithmetic and copies ran while one was open for 1% -> 2% of each run, Pallas kernels for 0% -> 0%
where the time goes in v1:
time: 1470 us; the launch traced here: 1460 us
  waiting for transfers between devices  720 us (49%)
  other arithmetic  313 us (21%)
  blocking collectives  148 us (10%)
  local copies, waits for them, and re-layouts  147 us (10%)
  matrix products  119 us (8%)
  between operations  15.1 us (1%)
    ppermute x30, waiting for transfers between devices, apply_graph(): parts.append(lax.ppermute(parts[-1], 'col', forward_2))  205 us
    reduce_scatter x2, waiting for transfers between devices, apply_graph(): lax.psum_scatter(col_totals.reshape(vec_width, -1), 'row', scatter_dimens...  202 us
    reduce_scatter x2, waiting for transfers between devices, apply_graph(): lax.psum_scatter(row_totals.reshape(vec_width, -1), 'col', scatter_dimens...  165 us
    scatter-add x14, other arithmetic, turn(): row_totals.at[:, row_index].add(forward)  160 us
    psum x1, waiting for transfers between devices, per_device(): lax.psum((product(basis, images), product(basis, basis)), ('row', 'col'))  148 us
    scatter-add x14, other arithmetic, turn(): col_totals.at[:, col_index].add(backward)  126 us
    psum x1, blocking collectives, per_device(): gram_x = lax.psum(product(block_x, block_x), ('row', 'col'))  68.9 us
    psum x1, blocking collectives, per_device(): rayleigh = lax.psum(product(orthonormal, image_x), ('row', 'col'))  65.5 us
  transfers between devices with their start and end apart: 36, of which 35 were waited for; matrix products, arithmetic and copies ran while one was open for 2% of the time, Pallas kernels for 0%

profile of v1, /device:TPU:1, one launch (start us, length us, event | category | flops | bytes accessed | tf_op | source)
XLA Modules:
  0.0 1463.1 jit_solution(14774851907993834700)
XLA Ops:
  8.4 68.9 %psum.28 = f32[64,64]{0,1:T(8,128)S(1)} all-reduce(f32[64,64]{0,1:T(8,128)S(1)} %convolution_multiply_fusion.3), channel_id=1, replica_groups=mesh['row'=8,'col'=16] {'row','col'}, use_global_device_ids=true, to_apply=%region_0.0 | all-reduce | flops 4096 | bytes 32768 | tf_op jit(solution)/shard_map/psum | solution.py:79
  93.1 7.6 collective-permute-done
  101.4 7.1 collective-permute-done.1
  109.3 7.2 collective-permute-done.2
  117.1 7.1 collective-permute-done.3
  124.9 7.1 collective-permute-done.4
  132.8 7.1 collective-permute-done.5
  140.6 8.2 collective-permute-done.6
  149.5 9.4 collective-permute-done.7
  159.7 8.6 collective-permute-done.8
  168.9 7.6 collective-permute-done.9
  177.3 7.1 collective-permute-done.10
  185.1 7.1 collective-permute-done.11
  193.0 7.1 collective-permute-done.12
  208.6 7.6 collective-permute-done.14
  230.9 291.5 %while.26 = (s32[]{:T(128)}, f32[128,96,128]{2,0,1:T(8,128)}, f32[128,48,128]{2,0,1:T(8,128)S(1)}, s32[]{:T(128)}, s32[576]{0:T(1024)S(1)}, /*index=5*/s32[]{:T(...) while((s32[]{:T(128)}, f32[128,96,128]{2,0,1:T(8,128)}, ...), condition=%wide.region_6.7_spmd.clone, body=%wide.region_3.6_spmd.clone.sunk | while | flops 543165312 | bytes 50343056 | solution.py:54
  241.2 13.6 scatter_fusion
  263.9 8.8 scatter_fusion.1
  282.8 13.7 scatter_fusion
  305.5 8.8 scatter_fusion.1
  324.4 13.7 scatter_fusion
  347.2 8.8 scatter_fusion.1
  366.1 13.7 scatter_fusion
  388.8 8.8 scatter_fusion.1
  407.8 13.7 scatter_fusion
  430.4 8.8 scatter_fusion.1
  449.4 13.6 scatter_fusion
  472.0 8.8 scatter_fusion.1
  491.0 13.6 scatter_fusion
  513.6 8.8 scatter_fusion.1
  530.6 115.1 %reduce-scatter.7.cloned.1.call-done = f32[128,768]{1,0:T(8,128)} async-done(((f32[128,6144]{1,0:T(8,128)}), f32[128,768]{1,0:T(8,128)}) %reduce-scatter.7.cloned.1.call-update) | async-done | bytes 393232 | tf_op jit(solution)/shard_map/reduce_scatter | solution.py:58
  645.7 85.5 %reduce-scatter.5.cloned.1.call-done = f32[128,768]{1,0:T(8,128)} async-done(((f32[128,12288]{1,0:T(8,128)}), f32[128,768]{1,0:T(8,128)}) %reduce-scatter.5.cloned.1.call-update) | async-done | bytes 393232 | tf_op jit(solution)/shard_map/reduce_scatter | solution.py:55
  732.7 65.5 %psum.29 = f32[64,64]{0,1:T(8,128)S(1)} all-reduce(f32[64,64]{0,1:T(8,128)S(1)} %convolution_multiply_fusion.2), channel_id=1, replica_groups=mesh['row'=8,'col'=16] {'row','col'}, use_global_device_ids=true, to_apply=%region_9.10 | all-reduce | flops 4096 | bytes 32768 | tf_op jit(solution)/shard_map/psum | solution.py:89
  799.2 14.0 all_gather.7
  814.4 6.4 collective-permute-done.15
  828.2 6.1 collective-permute-done.17
  835.0 6.1 collective-permute-done.18
  841.8 6.1 collective-permute-done.19
  848.6 6.1 collective-permute-done.20
  855.4 6.4 collective-permute-done.21
  862.5 7.2 collective-permute-done.22
  870.3 6.1 collective-permute-done.23
  877.1 6.1 collective-permute-done.24
  897.4 6.1 collective-permute-done.27
  904.2 6.2 collective-permute-done.28
  911.1 7.3 collective-permute-done.29
  928.6 200.9 %while.27 = (s32[]{:T(128)}, f32[64,96,128]{2,0,1:T(8,128)}, f32[64,48,128]{2,0,1:T(8,128)}, s32[]{:T(128)}, s32[576]{0:T(1024)S(1)}, /*index=5*/s32[]{:T(128)},...) while((s32[]{:T(128)}, f32[64,96,128]{2,0,1:T(8,128)}, ...), condition=%wide.region_13.14_spmd.clone, body=%wide.region_10.13_spmd.clone.sunk | while | flops 272632704 | bytes 27274384 | solution.py:54
  934.4 9.1 scatter_fusion.2
  948.0 9.2 scatter_fusion.3
  963.0 9.1 scatter_fusion.2
  976.7 9.2 scatter_fusion.3
  991.7 9.1 scatter_fusion.2
  1005.3 9.2 scatter_fusion.3
  1020.3 9.2 scatter_fusion.2
  1034.1 9.4 scatter_fusion.3
  1049.3 9.3 scatter_fusion.2
  1063.1 9.1 scatter_fusion.3
  1078.0 9.1 scatter_fusion.2
  1091.6 9.1 scatter_fusion.3
  1106.6 9.1 scatter_fusion.2
  1120.2 9.2 scatter_fusion.3
  1136.6 87.0 %reduce-scatter.11.cloned.1.call-done = f32[64,768]{1,0:T(8,128)} async-done(((f32[64,6144]{1,0:T(8,128)}), f32[64,768]{1,0:T(8,128)}) %reduce-scatter.11.cloned.1.call-update) | async-done | bytes 196624 | tf_op jit(solution)/shard_map/reduce_scatter | solution.py:58
  1223.6 79.0 %reduce-scatter.9.cloned.1.call-done = f32[64,768]{1,0:T(8,128)} async-done(((f32[64,12288]{1,0:T(8,128)}), f32[64,768]{1,0:T(8,128)}) %reduce-scatter.9.cloned.1.call-update) | async-done | bytes 196624 | tf_op jit(solution)/shard_map/reduce_scatter | solution.py:55
  1305.0 148.0 %all-reduce.3.cloned.1.call-done = (f32[192,192]{1,0:T(8,128)}, f32[192,192]{1,0:T(8,128)}) async-done(((f32[192,192]{1,0:T(8,128)}, f32[192,192]{1,0:T(8,128)}), (f32[192,192]{1,0:T(8,128)}, f32[192,192]{1,0:T(8,128)})) %all-reduce.3.cloned.1.call-update) | async-done | bytes 294928 | tf_op jit(solution)/shard_map/psum | solution.py:97
  (251 shorter events, 315.7 us)
Async XLA Ops:
  7.2 0.9 copy-start
  7.2 85.1 %copy-start.8 = (s32[1,1,576]{2,1,0:T(1,128)S(1)}, s32[1,1,576]{2,1,0:T(1,128)}, u32[]{:S(2)}) copy-start(s32[1,1,576]{2,1,0:T(1,128)} %param.12) | copy-start | bytes 6916
  7.2 85.2 %copy-start.9 = (s32[1,1,576]{2,1,0:T(1,128)S(1)}, s32[1,1,576]{2,1,0:T(1,128)}, u32[]{:S(2)}) copy-start(s32[1,1,576]{2,1,0:T(1,128)} %param.13) | copy-start | bytes 6916
  7.2 193.6 %all-gather.2.cloned.1.call-start = ((), (), s32[]{:S(2)}) async-start(), calls=%async_computation.4 | async-start | bytes 1769472 | tf_op jit(solution)/shard_map/all_gather | solution.py:25
  91.5 554.1 %reduce-scatter.7.cloned.1.call-start = ((), (), s32[]{:S(2)}) async-start(), calls=%async_computation.6 | async-start | bytes 3538944 | tf_op jit(solution)/shard_map/reduce_scatter | solution.py:58
  91.6 9.2 collective-permute-start
  100.7 7.8 collective-permute-start.1
  108.6 7.8 collective-permute-start.2
  116.4 7.8 collective-permute-start.3
  124.2 7.8 collective-permute-start.4
  132.1 7.8 collective-permute-start.5
  139.9 8.9 collective-permute-start.6
  148.9 10.1 collective-permute-start.7
  159.0 9.3 collective-permute-start.8
  168.2 8.3 collective-permute-start.9
  176.6 7.8 collective-permute-start.10
  184.4 7.8 collective-permute-start.11
  192.3 7.8 collective-permute-start.12
  200.1 7.8 collective-permute-start.13
  207.9 8.3 collective-permute-start.14
  524.4 206.8 %reduce-scatter.5.cloned.1.call-start = ((), (), s32[]{:S(2)}) async-start(), calls=%async_computation.5 | async-start | bytes 6684672 | tf_op jit(solution)/shard_map/reduce_scatter | solution.py:55
  530.5 693.1 %reduce-scatter.11.cloned.1.call-start = ((), (), s32[]{:S(2)}) async-start(), calls=%async_computation.8 | async-start | bytes 1769472 | tf_op jit(solution)/shard_map/reduce_scatter | solution.py:58
  732.4 102.7 %copy-start.3 = (f32[128,768]{1,0:T(8,128)}, f32[128,768]{1,0:T(8,128)S(1)}, u32[]{:S(2)}) copy-start(f32[128,768]{1,0:T(8,128)S(1)} %add.144) | copy-start | bytes 1179652
  813.2 7.6 collective-permute-start.15
  820.8 6.8 collective-permute-start.16
  827.6 6.8 collective-permute-start.17
  834.4 6.8 collective-permute-start.18
  841.2 6.8 collective-permute-start.19
  848.0 6.8 collective-permute-start.20
  854.7 7.1 collective-permute-start.21
  861.8 7.8 collective-permute-start.22
  869.6 6.8 collective-permute-start.23
  876.4 6.8 collective-permute-start.24
  883.2 6.8 collective-permute-start.25
  890.0 6.8 collective-permute-start.26
  896.8 6.8 collective-permute-start.27
  903.6 6.8 collective-permute-start.28
  910.4 8.0 collective-permute-start.29
  1129.4 2.9 copy-start.2
  1132.3 170.3 %reduce-scatter.9.cloned.1.call-start = ((), (), s32[]{:S(2)}) async-start(), calls=%async_computation.7 | async-start | bytes 3342336 | tf_op jit(solution)/shard_map/reduce_scatter | solution.py:55
  1134.2 0.9 copy-start.5
  1134.2 1.0 copy-start.6
  1134.2 2.4 copy-start.4
  1134.2 318.8 %all-reduce.3.cloned.1.call-start = ((), (), s32[]{:S(2)}) async-start(), calls=%async_computation.9 | async-start | bytes 786432 | tf_op jit(solution)/shard_map/psum | solution.py:97
  1135.2 321.0 %copy-start.1 = (f32[64,768]{1,0:T(8,128)S(1)}, f32[64,768]{1,0:T(8,128)}, u32[]{:S(2)}) copy-start(f32[64,768]{1,0:T(8,128)} %param.10) | copy-start | bytes 589828
  1303.6 152.6 %copy-start.7 = (f32[64,768]{1,0:T(8,128)}, f32[64,768]{1,0:T(8,128)S(1)}, u32[]{:S(2)}) copy-start(f32[64,768]{1,0:T(8,128)S(1)} %add.145) | copy-start | bytes 589828
Sparse Core Ops, SparseCore 0:
  91.6 21.1 all-gather.1
  524.5 121.1 reduce-scatter.6
  649.1 82.0 reduce-scatter.4
  1132.4 91.1 reduce-scatter.10
  1226.8 75.7 reduce-scatter.8
  1307.8 145.1 all-reduce.2
